TPU v7x, 32 devices: a whole 2x2x4 slice. The times are simulated.
32 devices in a mesh: rows: 8 (over y, x, core), grp: 4 (over z).
Axes of the slice: x: 2, y: 2, z: 4, core: 2. Of those that a mesh axis runs over, the one named last changes fastest.
Arguments:
- embeddings: bfloat16 [65536, 1024], P('rows', 'grp'), may hold values from -6 to 6
- fine_local: int32 [65536], P('rows'), may hold values from 0 to 2047
- send_counts: int32 [8, 8], P('rows'), may hold values from 0 to 2048, as said below
- old_fine: bfloat16 [16384, 1024], P('rows', 'grp'), may hold values from -6 to 6
- coarse_ids: int32 [16384], P('rows'), may hold values from 0 to 2047, as said below
- old_coarse: bfloat16 [2048, 1024], P('rows', 'grp'), may hold values from -6 to 6
Outputs:
- new_fine: bfloat16 [16384, 1024], P('rows', 'grp')
- coarse_dirs: bfloat16 [2048, 1024], P('rows')
Inputs may be any that keep to these rules, and one draw needn't show every extreme that they name: Row d of send_counts splits the 8192 rows of block d, in order, into segments for owners 0, 1, ...; each row of send_counts sums to 8192; one owner receives exactly 2048 rows from every block. `coarse_ids`: within each block of 2048 consecutive level-1 clusters, at most 512 have a level-2 cluster in any one block of 256 consecutive level-2 clusters; one such block reaches that from every block.
All inputs are finite; a program needn't handle non-finite values.
Results may differ from a plain program's by a relative error of at most 0.006.
Values may be sent and summed in bfloat16 or wider, within the bound.
A program may use at most 64 MiB of HBM per device.

v0:
```python
import math

import jax
import jax.numpy as jnp
from jax import lax
from jax.sharding import PartitionSpec as P


def onehot_sums(arrived, arrived_labels, fine_dev):
    slot_total = arrived.shape[0]
    width = arrived.shape[1]
    block_rows = math.gcd(slot_total, 2048)
    block_count = slot_total // block_rows
    cluster_index = jnp.arange(fine_dev, dtype=jnp.int32)

    def accumulate(state_pair, pieces):
        fine_sums, totals = state_pair
        row_block, label_block = pieces
        onehot = cluster_index[:, None] == label_block[None, :]
        fine_sums = fine_sums + jnp.dot(
            onehot.astype(jnp.bfloat16), row_block, preferred_element_type=jnp.float32
        )
        totals = totals + jnp.sum(onehot.astype(jnp.int32), axis=1)
        return ((fine_sums, totals), None)

    start_state = (jnp.zeros((fine_dev, width), jnp.float32), jnp.zeros((fine_dev,), jnp.int32))
    (fine_sums, totals), _ = lax.scan(
        accumulate,
        start_state,
        (
            arrived.reshape(block_count, block_rows, width),
            arrived_labels.reshape(block_count, block_rows),
        ),
    )
    return (fine_sums, totals.astype(jnp.float32))


def on_device(embeddings, fine_local, send_counts, old_fine, coarse_ids, old_coarse):
    peer_count = lax.axis_size("rows")
    per_dev = embeddings.shape[0]
    quarter = embeddings.shape[1]
    fine_dev = old_fine.shape[0]
    coarse_dev = old_coarse.shape[0]
    capacity = 2 * per_dev // peer_count
    counts = send_counts[0]
    starts = jnp.cumsum(counts) - counts
    offset = jnp.arange(capacity, dtype=jnp.int32)
    is_live = offset[None, :] < counts[:, None]
    padded_rows = jnp.concatenate(
        [embeddings, jnp.zeros((capacity, quarter), jnp.bfloat16)], axis=0
    )
    padded_local = jnp.concatenate([fine_local, jnp.zeros((capacity,), jnp.int32)], axis=0)

    def take_segment(first_row):
        segment_rows = lax.dynamic_slice_in_dim(padded_rows, first_row, capacity, 0)
        segment_labels = lax.dynamic_slice_in_dim(padded_local, first_row, capacity, 0)
        return (segment_rows, segment_labels)

    outgoing, raw_labels = lax.map(take_segment, starts)
    outgoing = jnp.where(is_live[:, :, None], outgoing, jnp.zeros((), jnp.bfloat16))
    labels = jnp.where(is_live, raw_labels, -1)
    arrived, arrived_labels = (
        lax.all_to_all(outgoing, "rows", split_axis=0, concat_axis=0, tiled=True),
        lax.all_to_all(labels, "rows", split_axis=0, concat_axis=0, tiled=True),
    )
    fine_sums, totals = onehot_sums(
        arrived.reshape(-1, quarter), arrived_labels.reshape(-1), fine_dev
    )
    new_fine = ((fine_sums + old_fine.astype(jnp.float32)) / (totals + 1.0)[:, None]).astype(
        jnp.bfloat16
    )
    owners = coarse_ids // coarse_dev
    local_id = coarse_ids - owners * coarse_dev
    capacity_two = 2 * fine_dev // peer_count
    member = (owners[:, None] == jnp.arange(peer_count, dtype=jnp.int32)[None, :]).astype(jnp.int32)
    slot_rank = jnp.sum(jnp.cumsum(member, axis=0) * member, axis=1) - 1
    slot_pos = owners * capacity_two + slot_rank
    placement = (
        jnp.arange(peer_count * capacity_two, dtype=jnp.int32)[:, None] == slot_pos[None, :]
    ).astype(jnp.bfloat16)
    outgoing_two = jnp.dot(placement, new_fine, preferred_element_type=jnp.float32).astype(
        jnp.bfloat16
    )
    label_plus = jnp.dot(
        placement, (local_id + 1).astype(jnp.bfloat16), preferred_element_type=jnp.float32
    )
    labels_two = label_plus.astype(jnp.int32) - 1
    received, received_labels = (
        lax.all_to_all(
            outgoing_two.reshape(peer_count, capacity_two, quarter),
            "rows",
            split_axis=0,
            concat_axis=0,
            tiled=True,
        ),
        lax.all_to_all(
            labels_two.reshape(peer_count, capacity_two),
            "rows",
            split_axis=0,
            concat_axis=0,
            tiled=True,
        ),
    )
    onehot_two = (
        jnp.arange(coarse_dev, dtype=jnp.int32)[:, None] == received_labels.reshape(-1)[None, :]
    )
    coarse_sums = jnp.dot(
        onehot_two.astype(jnp.bfloat16),
        received.reshape(-1, quarter),
        preferred_element_type=jnp.float32,
    )
    coarse_totals = jnp.sum(onehot_two.astype(jnp.int32), axis=1).astype(jnp.float32)
    coarse_means = (coarse_sums + old_coarse.astype(jnp.float32)) / (coarse_totals + 1.0)[:, None]
    squares = lax.psum(jnp.sum(coarse_means * coarse_means, axis=1), "grp")
    total_width = quarter * lax.axis_size("grp")
    unit_part = (coarse_means * lax.rsqrt(squares / total_width + 1e-06)[:, None]).astype(
        jnp.bfloat16
    )
    coarse_dirs = lax.all_gather(unit_part, "grp", axis=1, tiled=True)
    return (new_fine, coarse_dirs)


def solution(mesh):
    in_specs = (
        P("rows", "grp"),
        P("rows"),
        P("rows", None),
        P("rows", "grp"),
        P("rows"),
        P("rows", "grp"),
    )
    out_specs = (P("rows", "grp"), P("rows", None))
    return jax.shard_map(
        on_device, mesh=mesh, in_specs=in_specs, out_specs=out_specs, check_vma=False
    )
```

profile of v0, /device:TPU:0, one launch (start us, length us, event | category | flops | bytes accessed | tf_op | source)
XLA Modules:
  0.0 288.9 jit_solution(14380558250200745432)
XLA Ops:
  0.6 0.8 concatenate.7
  1.4 0.8 reduce-window.19
  2.2 0.7 bitcast_subtract_fusion
  2.9 4.6 %concatenate.6 = bf16[10240,256]{1,0:T(8,128)(2,1)} pad(bf16[8192,256]{1,0:T(8,128)(2,1)} %param.10, bf16[]{:T(256)} %constant.40.clone.1), padding=0_2048x0_0 | pad | bytes 9437186 | tf_op jit(solution)/shard_map/concatenate | solution.py:49
  7.5 40.4 %while.27 = (s32[]{:T(128)}, bf16[8,2048,256]{2,1,0:T(8,128)(2,1)}, s32[8,2048]{1,0:T(8,128)S(1)}, s32[8]{0:T(128)S(1)}, bf16[10240,256]{1,0:T(8,128)(2,1)}, /*index=5*/s32[10240]{0:T(1024)S(1)}) while((s32[]{:T(128)}, bf16[8,2048,256]{2,1,0:T(8,128)(2,1)}, s32[8,2048]{1,0:T(8,128)S(1)}, s32[8]{0:T(128)S(1)}, ...), condition=%wide.region_2.3_spmd.clone, body=%wide.region_1.2_spmd.sunk.clone | while | flops 5 | bytes 2130559 | solution.py:59
  9.8 2.5 bitcast_dynamic-update-slice_fusion.3
  14.8 2.5 bitcast_dynamic-update-slice_fusion.3
  17.6 0.6 dynamic_slice.37
  19.9 2.5 bitcast_dynamic-update-slice_fusion.3
  25.0 2.5 bitcast_dynamic-update-slice_fusion.3
  30.0 2.5 bitcast_dynamic-update-slice_fusion.3
  35.0 2.5 bitcast_dynamic-update-slice_fusion.3
  40.1 2.5 bitcast_dynamic-update-slice_fusion.3
  45.2 2.5 bitcast_dynamic-update-slice_fusion.3
  48.0 0.7 all_to_all.20
  48.7 5.2 %all-to-all-start = ((s32[8,1,2048]{2,1,0:T(1,128)}), s32[8,1,2048]{2,1,0:T(1,128)S(1)}, u32[]{:S(2)}, u32[]{:S(2)}) async-start(s32[8,1,2048]{2,1,0:T(1,128)} %all_to_all.20), calls=%async_computation | async-start | bytes 131072 | tf_op jit(solution)/shard_map/all_to_all | solution.py:64
  53.9 8.0 %broadcast_select_fusion = bf16[8,2048,256]{2,1,0:T(8,128)(2,1)} fusion(bf16[8,2048,256]{2,1,0:T(8,128)(2,1)} %get-tuple-element.69, pred[8,2048]{1,0:T(8,128)(4,1)S(1)} %iota_compare_fusion.17), kind=kLoop, calls=%fused_computation.18 | loop fusion | flops 4194304 | bytes 16793600 | tf_op jit(solution)/shard_map/jit(_where)/select_n | solution.py:60
  62.0 5.1 %all-to-all-start.1 = ((bf16[8,2048,256]{2,1,0:T(8,128)(2,1)}), bf16[8,2048,256]{2,1,0:T(8,128)(2,1)}, u32[]{:S(2)}, u32[]{:S(2)}) async-start(bf16[8,2048,256]{2,1,0:T(8,128)(2,1)} %broadcast_select_fusion), calls=%async_computation.1 | async-start | bytes 16777216 | tf_op jit(solution)/shard_map/all_to_all | solution.py:63
  67.1 2.3 reduce-window.20
  70.1 5.6 %fusion.11 = f32[1,4096]{1,0:T(1,128)S(1)} fusion(bf16[2048,1]{0,1:T(2,128)(2,1)S(1)} %reshape.98, s32[2048]{0:T(1024)S(1)} %get-tuple-element.123), kind=kOutput, calls=%fused_computation.15 | convolution fusion | flops 25165824 | bytes 28672 | tf_op jit(solution)/shard_map/dot_general | solution.py:84
  75.7 0.6 convert_add_fusion
  76.3 84.8 %all-to-all-done.1 = bf16[8,2048,256]{2,1,0:T(8,128)(2,1)} async-done(((bf16[8,2048,256]{2,1,0:T(8,128)(2,1)}), bf16[8,2048,256]{2,1,0:T(8,128)(2,1)}, u32[]{:S(2)}, u32[]{:S(2)}) %all-to-all-start.1) | async-done | bytes 8388640 | tf_op jit(solution)/shard_map/all_to_all | solution.py:63
  161.1 3.5 %all-to-all-start.2 = ((s32[8,1,512]{2,1,0:T(1,128)}), s32[8,1,512]{2,1,0:T(1,128)S(1)}, u32[]{:S(2)}, u32[]{:S(2)}) async-start(s32[8,1,512]{2,1,0:T(1,128)} %bitcast.9), calls=%async_computation.2 | async-start | bytes 32768 | tf_op jit(solution)/shard_map/all_to_all | solution.py:96
  164.7 54.2 %while.28 = (s32[]{:T(128)}, f32[2048,256]{1,0:T(8,128)S(1)}, s32[2048]{0:T(1024)S(1)}, s32[8,2048]{1,0:T(8,128)S(1)}, bf16[8,2048,256]{2,1,0:T(8,128)(2,1)}) while((s32[]{:T(128)}, f32[2048,256]{1,0:T(8,128)S(1)}, s32[2048]{0:T(1024)S(1)}, s32[8,2048]{1,0:T(8,128)S(1)}, bf16[8,2048,256]{2,1,0:T(8,128)(2,1)}) %tuple.58), condition=%wide.region_5.6_spmd.clone.clone, body=%wide.region_3.5_spmd.clone.sunk.clone | while | flops 2165311488 | bytes 5309004 | solution.py:27
  164.7 5.1 %fusion.35 = f32[2048,256]{1,0:T(8,128)S(1)} fusion(s32[2048]{0:T(1024)S(1)} %bitcast.59, f32[2048,256]{1,0:T(8,128)S(1)} %get-tuple-element.249, bf16[8,2048,256]{2,1,0:T(8,128)(2,1)} %get-tuple-element.257, s32[]{:T(128)} %get-tuple-element.248, pred[]{:T(512)S(6)} %compare.8), kind=kOutput, calls=%fused_computation.7.clone.1.clone | convolution fusion | flops 2152726528 | bytes 5251585 | tf_op jit(solution)/shard_map/while/body/eval_jaxpr/dot_general | solution.py:20
  169.8 1.7 fusion.36
  171.6 5.0 %fusion.35 = f32[2048,256]{1,0:T(8,128)S(1)} fusion(s32[2048]{0:T(1024)S(1)} %bitcast.59, f32[2048,256]{1,0:T(8,128)S(1)} %get-tuple-element.249, bf16[8,2048,256]{2,1,0:T(8,128)(2,1)} %get-tuple-element.257, s32[]{:T(128)} %get-tuple-element.248, pred[]{:T(512)S(6)} %compare.8), kind=kOutput, calls=%fused_computation.7.clone.1.clone | convolution fusion | flops 2152726528 | bytes 5251585 | tf_op jit(solution)/shard_map/while/body/eval_jaxpr/dot_general | solution.py:20
  176.6 1.7 fusion.36
  178.3 5.0 %fusion.35 = f32[2048,256]{1,0:T(8,128)S(1)} fusion(s32[2048]{0:T(1024)S(1)} %bitcast.59, f32[2048,256]{1,0:T(8,128)S(1)} %get-tuple-element.249, bf16[8,2048,256]{2,1,0:T(8,128)(2,1)} %get-tuple-element.257, s32[]{:T(128)} %get-tuple-element.248, pred[]{:T(512)S(6)} %compare.8), kind=kOutput, calls=%fused_computation.7.clone.1.clone | convolution fusion | flops 2152726528 | bytes 5251585 | tf_op jit(solution)/shard_map/while/body/eval_jaxpr/dot_general | solution.py:20
  183.3 1.7 fusion.36
  185.1 5.0 %fusion.35 = f32[2048,256]{1,0:T(8,128)S(1)} fusion(s32[2048]{0:T(1024)S(1)} %bitcast.59, f32[2048,256]{1,0:T(8,128)S(1)} %get-tuple-element.249, bf16[8,2048,256]{2,1,0:T(8,128)(2,1)} %get-tuple-element.257, s32[]{:T(128)} %get-tuple-element.248, pred[]{:T(512)S(6)} %compare.8), kind=kOutput, calls=%fused_computation.7.clone.1.clone | convolution fusion | flops 2152726528 | bytes 5251585 | tf_op jit(solution)/shard_map/while/body/eval_jaxpr/dot_general | solution.py:20
  190.1 1.7 fusion.36
  191.9 5.0 %fusion.35 = f32[2048,256]{1,0:T(8,128)S(1)} fusion(s32[2048]{0:T(1024)S(1)} %bitcast.59, f32[2048,256]{1,0:T(8,128)S(1)} %get-tuple-element.249, bf16[8,2048,256]{2,1,0:T(8,128)(2,1)} %get-tuple-element.257, s32[]{:T(128)} %get-tuple-element.248, pred[]{:T(512)S(6)} %compare.8), kind=kOutput, calls=%fused_computation.7.clone.1.clone | convolution fusion | flops 2152726528 | bytes 5251585 | tf_op jit(solution)/shard_map/while/body/eval_jaxpr/dot_general | solution.py:20
  196.9 1.7 fusion.36
  198.6 5.0 %fusion.35 = f32[2048,256]{1,0:T(8,128)S(1)} fusion(s32[2048]{0:T(1024)S(1)} %bitcast.59, f32[2048,256]{1,0:T(8,128)S(1)} %get-tuple-element.249, bf16[8,2048,256]{2,1,0:T(8,128)(2,1)} %get-tuple-element.257, s32[]{:T(128)} %get-tuple-element.248, pred[]{:T(512)S(6)} %compare.8), kind=kOutput, calls=%fused_computation.7.clone.1.clone | convolution fusion | flops 2152726528 | bytes 5251585 | tf_op jit(solution)/shard_map/while/body/eval_jaxpr/dot_general | solution.py:20
  203.6 1.7 fusion.36
  205.4 5.0 %fusion.35 = f32[2048,256]{1,0:T(8,128)S(1)} fusion(s32[2048]{0:T(1024)S(1)} %bitcast.59, f32[2048,256]{1,0:T(8,128)S(1)} %get-tuple-element.249, bf16[8,2048,256]{2,1,0:T(8,128)(2,1)} %get-tuple-element.257, s32[]{:T(128)} %get-tuple-element.248, pred[]{:T(512)S(6)} %compare.8), kind=kOutput, calls=%fused_computation.7.clone.1.clone | convolution fusion | flops 2152726528 | bytes 5251585 | tf_op jit(solution)/shard_map/while/body/eval_jaxpr/dot_general | solution.py:20
  210.4 1.7 fusion.36
  212.2 5.0 %fusion.35 = f32[2048,256]{1,0:T(8,128)S(1)} fusion(s32[2048]{0:T(1024)S(1)} %bitcast.59, f32[2048,256]{1,0:T(8,128)S(1)} %get-tuple-element.249, bf16[8,2048,256]{2,1,0:T(8,128)(2,1)} %get-tuple-element.257, s32[]{:T(128)} %get-tuple-element.248, pred[]{:T(512)S(6)} %compare.8), kind=kOutput, calls=%fused_computation.7.clone.1.clone | convolution fusion | flops 2152726528 | bytes 5251585 | tf_op jit(solution)/shard_map/while/body/eval_jaxpr/dot_general | solution.py:20
  217.2 1.7 fusion.36
  219.4 1.0 copy-done.1
  220.3 7.4 %fusion.14 = bf16[4096,256]{1,0:T(8,128)(2,1)} fusion(bf16[2048,256]{1,0:T(8,128)(2,1)S(1)} %divide_convert_fusion, s32[2048]{0:T(1024)S(1)} %get-tuple-element.123), kind=kOutput, calls=%fused_computation.19 | convolution fusion | flops 4304404480 | bytes 3153920 | tf_op jit(solution)/shard_map/dot_general | solution.py:81
  227.8 4.0 %all-to-all-start.3 = ((bf16[8,512,256]{2,1,0:T(8,128)(2,1)}), bf16[8,512,256]{2,1,0:T(8,128)(2,1)S(1)}, u32[]{:S(2)}, u32[]{:S(2)}) async-start(bf16[8,512,256]{2,1,0:T(8,128)(2,1)} %bitcast.57), calls=%async_computation.3 | async-start | bytes 4194304 | tf_op jit(solution)/shard_map/all_to_all | solution.py:89
  232.4 26.0 %all-to-all-done.3 = bf16[8,512,256]{2,1,0:T(8,128)(2,1)S(1)} async-done(((bf16[8,512,256]{2,1,0:T(8,128)(2,1)}), bf16[8,512,256]{2,1,0:T(8,128)(2,1)S(1)}, u32[]{:S(2)}, u32[]{:S(2)}) %all-to-all-start.3) | async-done | bytes 2097184 | tf_op jit(solution)/shard_map/all_to_all | solution.py:89
  258.5 1.3 multiply_reduce_fusion
  259.7 12.1 %psum.7 = f32[256]{0:T(256)S(1)} all-reduce(f32[256]{0:T(256)S(1)} %get-tuple-element.126), channel_id=1, replica_groups=mesh['rows'=8,'grp'=4] {'grp'}, use_global_device_ids=true, to_apply=%region_11.12 | all-reduce | flops 256 | bytes 2048 | tf_op jit(solution)/shard_map/psum | solution.py:114
  271.9 16.0 %all_gather.3 = bf16[256,1024]{0,1:T(8,128)(2,1)S(1)} all-gather(bf16[256,256]{0,1:T(8,128)(2,1)S(1)} %multiply_convert_fusion), channel_id=1, replica_groups=mesh['rows'=8,'grp'=4] {'grp'}, dimensions={1}, use_global_device_ids=true | all-gather | bytes 655360 | tf_op jit(solution)/shard_map/all_gather | solution.py:119
  287.9 1.0 copy.15
  (72 shorter events, 8.0 us)
Async XLA Ops:
  7.5 40.5 %copy-start.4 = (s32[1,8]{1,0:T(1,128)S(1)}, s32[1,8]{1,0:T(1,128)}, u32[]{:S(2)}) copy-start(s32[1,8]{1,0:T(1,128)} %param.12) | copy-start | bytes 100
  48.7 13.3 %all-to-all-start = ((s32[8,1,2048]{2,1,0:T(1,128)}), s32[8,1,2048]{2,1,0:T(1,128)S(1)}, u32[]{:S(2)}, u32[]{:S(2)}) async-start(s32[8,1,2048]{2,1,0:T(1,128)} %all_to_all.20), calls=%async_computation | async-start | bytes 131072 | tf_op jit(solution)/shard_map/all_to_all | solution.py:64
  62.0 5.1 %copy-start.3 = (s32[2048]{0:T(1024)S(1)}, s32[2048]{0:T(1024)}, u32[]{:S(2)}) copy-start(s32[2048]{0:T(1024)} %param.14) | copy-start | bytes 24580
  62.0 99.2 %all-to-all-start.1 = ((bf16[8,2048,256]{2,1,0:T(8,128)(2,1)}), bf16[8,2048,256]{2,1,0:T(8,128)(2,1)}, u32[]{:S(2)}, u32[]{:S(2)}) async-start(bf16[8,2048,256]{2,1,0:T(8,128)(2,1)} %broadcast_select_fusion), calls=%async_computation.1 | async-start | bytes 16777216 | tf_op jit(solution)/shard_map/all_to_all | solution.py:63
  161.1 66.6 %all-to-all-start.2 = ((s32[8,1,512]{2,1,0:T(1,128)}), s32[8,1,512]{2,1,0:T(1,128)S(1)}, u32[]{:S(2)}, u32[]{:S(2)}) async-start(s32[8,1,512]{2,1,0:T(1,128)} %bitcast.9), calls=%async_computation.2 | async-start | bytes 32768 | tf_op jit(solution)/shard_map/all_to_all | solution.py:96
  164.7 54.3 %copy-start = (bf16[2048,256]{1,0:T(8,128)(2,1)S(1)}, bf16[2048,256]{1,0:T(8,128)(2,1)}, u32[]{:S(2)}) copy-start(bf16[2048,256]{1,0:T(8,128)(2,1)} %param.13) | copy-start | bytes 3145732
  219.3 1.0 copy-start.1
  227.8 4.1 %copy-start.2 = (bf16[256,256]{1,0:T(8,128)(2,1)S(1)}, bf16[256,256]{1,0:T(8,128)(2,1)}, u32[]{:S(2)}) copy-start(bf16[256,256]{1,0:T(8,128)(2,1)} %param.15) | copy-start | bytes 393220
  227.8 30.7 %all-to-all-start.3 = ((bf16[8,512,256]{2,1,0:T(8,128)(2,1)}), bf16[8,512,256]{2,1,0:T(8,128)(2,1)S(1)}, u32[]{:S(2)}, u32[]{:S(2)}) async-start(bf16[8,512,256]{2,1,0:T(8,128)(2,1)} %bitcast.57), calls=%async_computation.3 | async-start | bytes 4194304 | tf_op jit(solution)/shard_map/all_to_all | solution.py:89
where the time goes:
time: 290 us; the launch traced here: 289 us
  waiting for transfers between devices  111 us (38%)
  matrix products  54.2 us (19%)
  local copies, waits for them, and re-layouts  35 us (12%)
  blocking collectives  28.1 us (10%)
  other arithmetic  27.8 us (10%)
  starting transfers between devices  17.8 us (6%)
  loops' own time  14.2 us (5%)
    all_to_all x1, waiting for transfers between devices, on_device(): lax.all_to_all(outgoing, 'rows', split_axis=0, concat_axis=0, tiled=True)  84.8 us
    dot_general x8, matrix products, accumulate(): jnp.dot(onehot.astype(jnp.bfloat16), row_block, preferred_element_type=jn...  39.9 us
    all_to_all x1, waiting for transfers between devices, on_device(): lax.all_to_all(outgoing_two.reshape(peer_count, capacity_two, quarter), '...  26 us
    dynamic_update_slice x16, local copies, waits for them, and re-layouts, on_device(): outgoing, raw_labels = lax.map(take_segment, starts)  21.2 us
    all_gather x1, blocking collectives, on_device(): coarse_dirs = lax.all_gather(unit_part, 'grp', axis=1, tiled=True)  16 us
    another operation x1, loops' own time, on_device(): outgoing, raw_labels = lax.map(take_segment, starts)  13.9 us
    reduce_sum x8, other arithmetic, accumulate(): totals = totals + jnp.sum(onehot.astype(jnp.int32), axis=1)  13.9 us
    psum x1, blocking collectives, on_device(): squares = lax.psum(jnp.sum(coarse_means * coarse_means, axis=1), 'grp')  12.1 us
  transfers between devices with their start and end apart: 4, of which 2 were waited for; matrix products, arithmetic and copies ran while one was open for 28% of the time, Pallas kernels for 0%

commit v1 on v0

--- a/solution.py
+++ b/solution.py
@@ -1,9 +1,221 @@
+import functools
 import math
 
 import jax
 import jax.numpy as jnp
 from jax import lax
+from jax.experimental import pallas as pl
+from jax.experimental.pallas import tpu as pltpu
 from jax.sharding import PartitionSpec as P
+
+MESH = pl.DeviceIdType.MESH
+LANES = 128
+
+
+def neighbours(me):
+    core, x, y = me % 2, (me // 2) % 2, me // 4
+    other_x, other_y = 1 - x, 1 - y
+    partner = 1 - core + 2 * x + 4 * y
+    along = {
+        (0, 0): me,
+        (1, 0): core + 2 * other_x + 4 * y,
+        (0, 1): core + 2 * x + 4 * other_y,
+        (1, 1): core + 2 * other_x + 4 * other_y,
+    }
+    return partner, along
+
+
+def enter(targets):
+    barrier = pltpu.get_barrier_semaphore()
+    for target in targets:
+        pl.semaphore_signal(barrier, inc=1, device_id={"rows": target}, device_id_type=MESH)
+    pl.semaphore_wait(barrier, len(targets))
+
+
+FIRST = ((1, 1, 0), (1, 1, 1), (1, 0, 0), (0, 1, 1), (1, 0, 1), (0, 1, 0))
+
+
+def fine_kernel(
+    tiles,
+    emb,
+    gid,
+    first_tile,
+    old,
+    out,
+    other_emb,
+    other_gid,
+    other_first,
+    acc,
+    hits,
+    away,
+    landed,
+    counts,
+    own_counts,
+    landed_counts,
+    swap_send,
+    swap_recv,
+    meta_sem,
+    send_sem,
+    recv_sem,
+    count_send,
+    count_recv,
+):
+    me = lax.axis_index("rows")
+    partner, along = neighbours(me)
+    fine_dev = old.shape[0]
+    half = fine_dev // 2
+    label_rows = gid.shape[0] - 8
+    enter([partner, along[1, 0], along[0, 1], along[1, 1]])
+
+    def remote(src, dst, send, recv, target):
+        return pltpu.make_async_remote_copy(
+            src_ref=src,
+            dst_ref=dst,
+            send_sem=send,
+            recv_sem=recv,
+            device_id={"rows": target},
+            device_id_type=MESH,
+        )
+
+    swaps = [
+        remote(gid, other_gid, swap_send.at[0], swap_recv.at[0], partner),
+        remote(emb, other_emb, swap_send.at[1], swap_recv.at[1], partner),
+    ]
+    for copy in swaps:
+        copy.start()
+    swaps[0].wait_recv()
+    meta = pltpu.make_async_copy(other_gid.at[pl.ds(label_rows, 8)], other_first, meta_sem)
+    meta.start()
+    meta.wait()
+    swaps[1].wait_recv()
+
+    counts[...] = jnp.zeros_like(counts)
+    index = lax.broadcasted_iota(jnp.int32, (half, LANES), 0)
+
+    def sums(owner, part, total):
+        base = owner * fine_dev + part * half
+        start_a = first_tile[0, owner]
+        start_b = other_first[0, 0, owner]
+        total[...] = jnp.zeros_like(total)
+        hits[...] = jnp.zeros_like(hits)
+
+        @pl.loop(0, tiles)
+        def _(step):
+            tile_a = start_a + step
+            tile_b = start_b + step
+            hot_a = jnp.where(index == gid[tile_a] - base, 1.0, 0.0).astype(jnp.bfloat16)
+            hot_b = jnp.where(index == other_gid[tile_b] - base, 1.0, 0.0).astype(
+                jnp.bfloat16
+            )
+            rows_a = emb[tile_a]
+            rows_b = other_emb[tile_b]
+            total[...] += jnp.dot(
+                jnp.concatenate([hot_a, hot_b], axis=1),
+                jnp.concatenate([rows_a, rows_b], axis=0),
+                preferred_element_type=jnp.float32,
+            )
+            hits[...] += hot_a + hot_b
+
+        return lax.dot_general(
+            jnp.ones((8, LANES), jnp.bfloat16),
+            hits[...],
+            (((1,), (1,)), ((), ())),
+            preferred_element_type=jnp.float32,
+        )[0:1]
+
+    sends = []
+    for slot, (qx, qy, part) in enumerate(FIRST):
+        counts[pl.ds(slot, 1), :] = sums(along[qx, qy], part, acc.at[0])
+        if slot == 5:
+            count_copies = []
+            for place, (cx, cy) in enumerate(((1, 0), (0, 1), (1, 1))):
+                copy = remote(
+                    counts,
+                    landed_counts.at[place],
+                    count_send.at[place],
+                    count_recv.at[place],
+                    along[cx, cy],
+                )
+                copy.start()
+                count_copies.append(copy)
+        if slot >= 4:
+            sends[5 - slot].wait_recv()
+            away[slot] = (acc[0] + landed[5 - slot].astype(jnp.float32)).astype(jnp.bfloat16)
+        else:
+            away[slot] = acc[0].astype(jnp.bfloat16)
+        target = along[1, 0] if slot % 2 == 0 else along[0, 1]
+        copy = remote(away.at[slot], landed.at[slot], send_sem.at[slot], recv_sem.at[slot], target)
+        copy.start()
+        sends.append(copy)
+    for part in range(2):
+        own_counts[pl.ds(part, 1), :] = sums(me, part, acc.at[part])
+    for copy in count_copies:
+        copy.wait_recv()
+    for part in range(2):
+        seen = own_counts[pl.ds(part, 1), :]
+        for place, quad in enumerate(((1, 0), (0, 1), (1, 1))):
+            row = FIRST.index(quad + (part,))
+            seen = seen + landed_counts[place, pl.ds(row, 1), :]
+        divisor = jnp.broadcast_to(seen + 1.0, (LANES, half)).T
+        divisor = jnp.concatenate([divisor] * (old.shape[1] // LANES), axis=1)
+        near, far = (2, 5) if part == 0 else (3, 4)
+        sends[near].wait_recv()
+        sends[far].wait_recv()
+        span = pl.ds(part * half, half)
+        total = acc[part] + landed[near].astype(jnp.float32) + landed[far].astype(jnp.float32)
+        out[span, :] = ((total + old[span, :].astype(jnp.float32)) / divisor).astype(jnp.bfloat16)
+    for copy in swaps + sends + count_copies:
+        copy.wait_send()
+
+
+def fine_level(embeddings, fine_local, send_counts, old_fine):
+    peers = lax.axis_size("rows")
+    per_dev, width = embeddings.shape
+    fine_dev = old_fine.shape[0]
+    half = fine_dev // 2
+    capacity = 2 * per_dev // peers
+    tiles = capacity // LANES + 1
+    position = jnp.arange(per_dev, dtype=jnp.int32)
+    before = jnp.arange(peers)[None, :] < jnp.arange(peers)[:, None]
+    starts = jnp.sum(jnp.where(before, send_counts, 0), axis=1)
+    ends = starts + send_counts[0]
+    owner = jnp.sum((ends[:, None] <= position[None, :]).astype(jnp.int32), axis=0)
+    label_rows = per_dev // LANES
+    first_tile = jnp.minimum(starts // LANES, label_rows - tiles)[None, :]
+    gid = (owner * fine_dev + fine_local).reshape(label_rows, LANES)
+    gid = jnp.concatenate([gid, jnp.pad(first_tile, ((0, 7), (0, LANES - peers)))], axis=0)
+    gid = gid[:, None, :]
+    tiled = embeddings.reshape(label_rows, LANES, width)
+    vmem = pl.BlockSpec(memory_space=pltpu.VMEM)
+    dma = pltpu.SemaphoreType.DMA
+    return pl.pallas_call(
+        functools.partial(fine_kernel, tiles),
+        out_shape=jax.ShapeDtypeStruct(old_fine.shape, jnp.bfloat16),
+        in_specs=[vmem, vmem, pl.BlockSpec(memory_space=pltpu.SMEM), vmem],
+        out_specs=vmem,
+        scratch_shapes=[
+            pltpu.VMEM(tiled.shape, jnp.bfloat16),
+            pltpu.VMEM(gid.shape, jnp.int32),
+            pltpu.SMEM((8, 1, LANES), jnp.int32),
+            pltpu.VMEM((2, half, width), jnp.float32),
+            pltpu.VMEM((half, LANES), jnp.bfloat16),
+            pltpu.VMEM((6, half, width), jnp.bfloat16),
+            pltpu.VMEM((6, half, width), jnp.bfloat16),
+            pltpu.VMEM((8, half), jnp.float32),
+            pltpu.VMEM((8, half), jnp.float32),
+            pltpu.VMEM((3, 8, half), jnp.float32),
+            dma((2,)),
+            dma((2,)),
+            dma,
+            dma((6,)),
+            dma((6,)),
+            dma((3,)),
+            dma((3,)),
+        ],
+        compiler_params=pltpu.CompilerParams(
+            collective_id=0, has_side_effects=True, vmem_limit_bytes=48 * 1024 * 1024
+        ),
+    )(tiled, gid, first_tile, old_fine)
 
 
 def onehot_sums(arrived, arrived_labels, fine_dev):
@@ -35,12 +247,11 @@
     return (fine_sums, totals.astype(jnp.float32))
 
 
-def on_device(embeddings, fine_local, send_counts, old_fine, coarse_ids, old_coarse):
+def exchanged_rows(embeddings, fine_local, send_counts, old_fine):
     peer_count = lax.axis_size("rows")
     per_dev = embeddings.shape[0]
     quarter = embeddings.shape[1]
     fine_dev = old_fine.shape[0]
-    coarse_dev = old_coarse.shape[0]
     capacity = 2 * per_dev // peer_count
     counts = send_counts[0]
     starts = jnp.cumsum(counts) - counts
@@ -69,6 +280,17 @@
     new_fine = ((fine_sums + old_fine.astype(jnp.float32)) / (totals + 1.0)[:, None]).astype(
         jnp.bfloat16
     )
+    return new_fine
+
+
+def on_device(embeddings, fine_local, send_counts, old_fine, coarse_ids, old_coarse):
+    peer_count = lax.axis_size("rows")
+    quarter = embeddings.shape[1]
+    fine_dev = old_fine.shape[0]
+    coarse_dev = old_coarse.shape[0]
+    tree = peer_count == 8 and 2 * embeddings.shape[0] // peer_count >= fine_dev
+    level = fine_level if tree else exchanged_rows
+    new_fine = level(embeddings, fine_local, send_counts, old_fine)
     owners = coarse_ids // coarse_dev
     local_id = coarse_ids - owners * coarse_dev
     capacity_two = 2 * fine_dev // peer_count

time: 290 us -> 159 us (0.55)
  waiting for transfers between devices: 111 us -> 25.4 us
  Pallas kernels: 0 us -> 71.3 us
  matrix products: 54.2 us -> 15.6 us
  local copies, waits for them, and re-layouts: 35 us -> 2.39 us
  other arithmetic: 27.8 us -> 6.03 us
  loops' own time: 14.2 us -> 0 us
  starting transfers between devices: 17.8 us -> 8.91 us
    all_to_all x2 -> x0, waiting for transfers between devices: 84.9 us -> none  [the longest x1 84.8 us: on_device(): lax.all_to_all(outgoing, 'rows', split_axis=0, concat_axis=0, tiled=True)]
    pallas_call x0 -> x1, Pallas kernels: none -> 71.3 us  [fine_level(): pl.pallas_call(functools.partial(fine_kernel, tiles), out_shape=jax.Shape...]
    dot_general x8 -> x0, matrix products: 39.9 us -> none  [accumulate(): jnp.dot(onehot.astype(jnp.bfloat16), row_block, preferred_element_type=jn...]
    dynamic_update_slice x16 -> x0, local copies, waits for them, and re-layouts: 21.2 us -> none  [on_device(): outgoing, raw_labels = lax.map(take_segment, starts)]
    another operation x2 -> x0, loops' own time: 14.2 us -> none  [the longest x1 13.9 us: on_device(): outgoing, raw_labels = lax.map(take_segment, starts)]
    reduce_sum x8 -> x2, other arithmetic: 13.9 us -> 0.26 us  [the longest x1 0.15 us: fine_level(): jnp.sum((ends[:, None] <= position[None, :]).astype(jnp.int32), axis=0)]
    all_to_all x2 -> x0, starting transfers between devices: 10.3 us -> none  [the longest x1 5.17 us: on_device(): lax.all_to_all(labels, 'rows', split_axis=0, concat_axis=0, tiled=True)]
    select_n x2 -> x0, other arithmetic: 8.12 us -> none  [the longest x1 8.04 us: on_device(): jnp.where(is_live[:, :, None], outgoing, jnp.zeros((), jnp.bfloat16))]
  transfers between devices with their start and end apart: 4 -> 2, of which waited for: 2 -> 1; matrix products, arithmetic and copies ran while one was open for 28% -> 6% of each run, Pallas kernels for 0% -> 45%
where the time goes in v1:
time: 159 us; the launch traced here: 158 us
  Pallas kernels  71.3 us (45%)
  blocking collectives  28 us (18%)
  waiting for transfers between devices  25.4 us (16%)
  matrix products  15.6 us (10%)
  starting transfers between devices  8.91 us (6%)
  other arithmetic  6.03 us (4%)
  local copies, waits for them, and re-layouts  2.39 us (2%)
    pallas_call x1, Pallas kernels, fine_level(): pl.pallas_call(functools.partial(fine_kernel, tiles), out_shape=jax.Shape...  71.3 us
    all_to_all x1, waiting for transfers between devices, on_device(): lax.all_to_all(outgoing_two.reshape(peer_count, capacity_two, quarter), '...  25.4 us
    all_gather x1, blocking collectives, on_device(): coarse_dirs = lax.all_gather(unit_part, 'grp', axis=1, tiled=True)  15.9 us
    psum x1, blocking collectives, on_device(): squares = lax.psum(jnp.sum(coarse_means * coarse_means, axis=1), 'grp')  12.1 us
    dot_general x1, matrix products, on_device(): jnp.dot(placement, new_fine, preferred_element_type=jnp.float32)  7.47 us
    dot_general x1, matrix products, on_device(): jnp.dot(placement, (local_id + 1).astype(jnp.bfloat16), preferred_element...  5.59 us
    all_to_all x1, starting transfers between devices, on_device(): lax.all_to_all(labels_two.reshape(peer_count, capacity_two), 'rows', spli...  5.17 us
    all_to_all x1, starting transfers between devices, on_device(): lax.all_to_all(outgoing_two.reshape(peer_count, capacity_two, quarter), '...  3.73 us
  transfers between devices with their start and end apart: 2, of which 1 were waited for; matrix products, arithmetic and copies ran while one was open for 6% of the time, Pallas kernels for 45%

profile of v1, /device:TPU:0, one launch (start us, length us, event | category | flops | bytes accessed | tf_op | source)
XLA Modules:
  0.0 158.3 jit_solution(5250311272639678888)
XLA Ops:
  0.6 0.7 add_select_fusion
  1.3 2.3 %reduce-window.6 = s32[8,16,128]{2,1,0:T(8,128)S(1)} reduce-window(s32[8,16,128]{2,1,0:T(8,128)S(1)} %fusion.11, s32[]{:T(128)} %constant.40.clone.1), window={size=1x1x128 pad=0_0x0_0x127_0}, to_apply=%region_2.3 | reduce-window | flops 2080768 | bytes 131076 | tf_op jit(solution)/shard_map/reduce-window
  3.6 0.3 slice_reduce_fusion
  3.9 0.2 reduce-window.9
  4.1 0.1 add_bitcast_fusion
  4.2 0.7 add_convert_fusion
  5.0 0.0 copy-start.3
  5.0 0.0 copy-start.2
  5.0 0.0 copy-start
  5.0 5.6 %fusion.1 = f32[1,4096]{1,0:T(1,128)S(1)} fusion(bf16[2048,1]{0,1:T(2,128)(2,1)S(1)} %reshape.108, s32[2048]{0:T(1024)S(1)} %get-tuple-element.9), kind=kOutput, calls=%fused_computation.2 | convolution fusion | flops 25165824 | bytes 28672 | tf_op jit(solution)/shard_map/dot_general | solution.py:306
  10.6 0.6 convert_add_fusion
  11.2 5.2 %all-to-all-start = ((s32[8,1,512]{2,1,0:T(1,128)}), s32[8,1,512]{2,1,0:T(1,128)S(1)}, u32[]{:S(2)}, u32[]{:S(2)}) async-start(s32[8,1,512]{2,1,0:T(1,128)} %bitcast.8), calls=%async_computation | async-start | bytes 32768 | tf_op jit(solution)/shard_map/all_to_all | solution.py:318
  16.4 0.0 copy-done.3
  16.4 0.1 select_reduce_fusion
  16.5 0.1 convert_reduce_fusion.1
  16.7 0.0 copy-done.2
  16.7 0.0 copy-done
  16.7 71.3 %shard_map.77 = bf16[2048,256]{1,0:T(8,128)(2,1)S(1)} custom-call(bf16[64,128,256]{2,1,0:T(8,128)(2,1)} %bitcast.42, s32[72,1,128]{2,1,0:T(1,128)S(1)} %bitcast.41, s32[1,8]{1,0:T(1,128)S(1)} %fusion.14.first_tile, bf16[2048,256]{1,0:T(8,128)(2,1)S(1)} %copy-done), custom_call_target="tpu_custom_call" | custom-call | tf_op jit(solution)/shard_map/pallas_call | solution.py:191
  88.0 7.5 %fusion.4 = bf16[4096,256]{1,0:T(8,128)(2,1)} fusion(bf16[2048,256]{1,0:T(8,128)(2,1)S(1)} %shard_map.77, s32[2048]{0:T(1024)S(1)} %get-tuple-element.9), kind=kOutput, calls=%fused_computation.5 | convolution fusion | flops 4304404480 | bytes 3153920 | tf_op jit(solution)/shard_map/dot_general | solution.py:303
  95.5 0.0 copy-start.1
  95.5 0.0 all-to-all-done
  95.5 3.7 %all-to-all-start.1 = ((bf16[8,512,256]{2,1,0:T(8,128)(2,1)}), bf16[8,512,256]{2,1,0:T(8,128)(2,1)S(1)}, u32[]{:S(2)}, u32[]{:S(2)}) async-start(bf16[8,512,256]{2,1,0:T(8,128)(2,1)} %bitcast.44), calls=%async_computation.1 | async-start | bytes 4194304 | tf_op jit(solution)/shard_map/all_to_all | solution.py:311
  99.2 0.0 copy-done.1
  99.2 0.1 copy.12
  99.3 0.5 convert_reduce_fusion
  99.8 0.6 convert_add_fusion.1
  100.4 25.4 %all-to-all-done.1 = bf16[8,512,256]{2,1,0:T(8,128)(2,1)S(1)} async-done(((bf16[8,512,256]{2,1,0:T(8,128)(2,1)}), bf16[8,512,256]{2,1,0:T(8,128)(2,1)S(1)}, u32[]{:S(2)}, u32[]{:S(2)}) %all-to-all-start.1) | async-done | bytes 2097184 | tf_op jit(solution)/shard_map/all_to_all | solution.py:311
  125.8 2.5 %multiply_reduce_fusion = (f32[256]{0:T(256)}, f32[256,256]{0,1:T(8,128)S(1)}) fusion(f32[256]{0:T(256)} %convert_add_fusion.1, bf16[256,256]{0,1:T(8,128)(2,1)S(1)} %copy.12, bf16[4096,256]{1,0:T(8,128)(2,1)S(1)} %bitcast.43, s32[4096]{0:T(1024)S(1)} %bitcast.46), kind=kOutput, calls=%fused_computation.13 | convolution fusion | flops 538246912 | bytes 2508800 | tf_op jit(solution)/shard_map/dot_general | solution.py:329
  128.3 12.1 %psum.7 = f32[256]{0:T(256)S(1)} all-reduce(f32[256]{0:T(256)} %get-tuple-element.12), channel_id=1, replica_groups=mesh['rows'=8,'grp'=4] {'grp'}, use_global_device_ids=true, to_apply=%region_7.8 | all-reduce | flops 256 | bytes 2048 | tf_op jit(solution)/shard_map/psum | solution.py:336
  140.4 15.9 %all_gather.3 = bf16[256,1024]{0,1:T(8,128)(2,1)S(1)} all-gather(bf16[256,256]{0,1:T(8,128)(2,1)S(1)} %multiply_convert_fusion), channel_id=1, replica_groups=mesh['rows'=8,'grp'=4] {'grp'}, dimensions={1}, use_global_device_ids=true | all-gather | bytes 655360 | tf_op jit(solution)/shard_map/all_gather | solution.py:341
  156.4 1.0 copy.13
  157.4 1.0 copy.17
  (9 shorter events, 0.1 us)
Async XLA Ops:
  5.0 11.4 %copy-start.3 = (s32[1,8]{1,0:T(1,128)S(1)}, s32[1,8]{1,0:T(1,128)}, u32[]{:S(2)}) copy-start(s32[1,8]{1,0:T(1,128)} %param.8) | copy-start | bytes 100
  5.0 11.7 %copy-start.2 = (s32[8192]{0:T(1024)S(1)}, s32[8192]{0:T(1024)}, u32[]{:S(2)}) copy-start(s32[8192]{0:T(1024)} %param.7) | copy-start | bytes 98308
  5.0 11.7 %copy-start = (bf16[2048,256]{1,0:T(8,128)(2,1)S(1)}, bf16[2048,256]{1,0:T(8,128)(2,1)}, u32[]{:S(2)}) copy-start(bf16[2048,256]{1,0:T(8,128)(2,1)} %old.1) | copy-start | bytes 3145732
  11.2 84.3 %all-to-all-start = ((s32[8,1,512]{2,1,0:T(1,128)}), s32[8,1,512]{2,1,0:T(1,128)S(1)}, u32[]{:S(2)}, u32[]{:S(2)}) async-start(s32[8,1,512]{2,1,0:T(1,128)} %bitcast.8), calls=%async_computation | async-start | bytes 32768 | tf_op jit(solution)/shard_map/all_to_all | solution.py:318
  95.5 3.8 %copy-start.1 = (bf16[256,256]{1,0:T(8,128)(2,1)S(1)}, bf16[256,256]{1,0:T(8,128)(2,1)}, u32[]{:S(2)}) copy-start(bf16[256,256]{1,0:T(8,128)(2,1)} %param.11) | copy-start | bytes 393220
  95.5 30.3 %all-to-all-start.1 = ((bf16[8,512,256]{2,1,0:T(8,128)(2,1)}), bf16[8,512,256]{2,1,0:T(8,128)(2,1)S(1)}, u32[]{:S(2)}, u32[]{:S(2)}) async-start(bf16[8,512,256]{2,1,0:T(8,128)(2,1)} %bitcast.44), calls=%async_computation.1 | async-start | bytes 4194304 | tf_op jit(solution)/shard_map/all_to_all | solution.py:311

commit v2 on v1

--- a/solution.py
+++ b/solution.py
@@ -25,25 +25,28 @@
     return partner, along
 
 
-def enter(targets):
-    barrier = pltpu.get_barrier_semaphore()
-    for target in targets:
-        pl.semaphore_signal(barrier, inc=1, device_id={"rows": target}, device_id_type=MESH)
-    pl.semaphore_wait(barrier, len(targets))
-
-
 FIRST = ((1, 1, 0), (1, 1, 1), (1, 0, 0), (0, 1, 1), (1, 0, 1), (0, 1, 0))
-
-
-def fine_kernel(
+AWAY = ((1, 1), (1, 0), (0, 1))
+META = 8
+
+
+def one_hot(index, ids):
+    low = jnp.clip(ids, -1, index.shape[0]).astype(jnp.int16)
+    same = index == jnp.broadcast_to(low, index.shape)
+    return jnp.where(same, jnp.ones((), jnp.bfloat16), jnp.zeros((), jnp.bfloat16))
+
+
+def levels_kernel(
     tiles,
     emb,
-    gid,
+    ids,
     first_tile,
     old,
+    old_coarse,
     out,
+    dirs,
     other_emb,
-    other_gid,
+    other_ids,
     other_first,
     acc,
     hits,
@@ -52,6 +55,13 @@
     counts,
     own_counts,
     landed_counts,
+    other_fine,
+    coarse_away,
+    coarse_landed,
+    coarse_counts,
+    coarse_counts_landed,
+    means,
+    squares,
     swap_send,
     swap_recv,
     meta_sem,
@@ -59,63 +69,85 @@
     recv_sem,
     count_send,
     count_recv,
+    fine_send,
+    fine_recv,
+    coarse_send,
+    coarse_recv,
+    coarse_count_send,
+    coarse_count_recv,
+    means_send,
+    means_recv,
+    squares_send,
+    squares_recv,
 ):
     me = lax.axis_index("rows")
+    slab = lax.axis_index("grp")
+    slabs = lax.axis_size("grp")
     partner, along = neighbours(me)
-    fine_dev = old.shape[0]
+    fine_dev, width = old.shape
     half = fine_dev // 2
-    label_rows = gid.shape[0] - 8
-    enter([partner, along[1, 0], along[0, 1], along[1, 1]])
-
-    def remote(src, dst, send, recv, target):
+    coarse_dev = old_coarse.shape[0]
+    label_rows = emb.shape[0]
+    fine_tiles = out.shape[0]
+    others = [(slab + step) % slabs for step in range(1, slabs)]
+
+    barrier = pltpu.get_barrier_semaphore()
+    mates = [partner] + [along[quad] for quad in AWAY]
+    for mate in mates:
+        pl.semaphore_signal(barrier, inc=1, device_id={"rows": mate}, device_id_type=MESH)
+    for other in others:
+        pl.semaphore_signal(barrier, inc=1, device_id={"grp": other}, device_id_type=MESH)
+    pl.semaphore_wait(barrier, len(mates) + len(others))
+
+    def remote(src, dst, send, recv, target, axis="rows"):
         return pltpu.make_async_remote_copy(
             src_ref=src,
             dst_ref=dst,
             send_sem=send,
             recv_sem=recv,
-            device_id={"rows": target},
+            device_id={axis: target},
             device_id_type=MESH,
         )
 
     swaps = [
-        remote(gid, other_gid, swap_send.at[0], swap_recv.at[0], partner),
+        remote(ids, other_ids, swap_send.at[0], swap_recv.at[0], partner),
         remote(emb, other_emb, swap_send.at[1], swap_recv.at[1], partner),
     ]
     for copy in swaps:
         copy.start()
+    counts[...] = jnp.zeros_like(counts)
+    coarse_counts[...] = jnp.zeros_like(coarse_counts)
     swaps[0].wait_recv()
-    meta = pltpu.make_async_copy(other_gid.at[pl.ds(label_rows, 8)], other_first, meta_sem)
+    meta = pltpu.make_async_copy(other_ids.at[pl.ds(label_rows, META)], other_first, meta_sem)
     meta.start()
     meta.wait()
     swaps[1].wait_recv()
 
-    counts[...] = jnp.zeros_like(counts)
-    index = lax.broadcasted_iota(jnp.int32, (half, LANES), 0)
-
-    def sums(owner, part, total):
-        base = owner * fine_dev + part * half
-        start_a = first_tile[0, owner]
-        start_b = other_first[0, 0, owner]
-        total[...] = jnp.zeros_like(total)
-        hits[...] = jnp.zeros_like(hits)
-
-        @pl.loop(0, tiles)
+    index = lax.broadcasted_iota(jnp.int32, (half, LANES), 0).astype(jnp.int16)
+
+    def add_tiles(total, rows_of, ids_of, steps, depth):
+        def piece(tile):
+            hots, rows = [], []
+            for side in range(2):
+                hots.append(one_hot(index, ids_of(side, tile)))
+                rows.append(rows_of(side, tile))
+            hits[...] += hots[0] + hots[1]
+            return hots, rows
+
+        @pl.loop(0, steps)
         def _(step):
-            tile_a = start_a + step
-            tile_b = start_b + step
-            hot_a = jnp.where(index == gid[tile_a] - base, 1.0, 0.0).astype(jnp.bfloat16)
-            hot_b = jnp.where(index == other_gid[tile_b] - base, 1.0, 0.0).astype(
-                jnp.bfloat16
-            )
-            rows_a = emb[tile_a]
-            rows_b = other_emb[tile_b]
+            hots, rows = [], []
+            for part in range(depth):
+                more_hots, more_rows = piece(step * depth + part)
+                hots += more_hots
+                rows += more_rows
             total[...] += jnp.dot(
-                jnp.concatenate([hot_a, hot_b], axis=1),
-                jnp.concatenate([rows_a, rows_b], axis=0),
+                jnp.concatenate(hots, axis=1),
+                jnp.concatenate(rows, axis=0),
                 preferred_element_type=jnp.float32,
             )
-            hits[...] += hot_a + hot_b
-
+
+    def hit_row():
         return lax.dot_general(
             jnp.ones((8, LANES), jnp.bfloat16),
             hits[...],
@@ -123,18 +155,33 @@
             preferred_element_type=jnp.float32,
         )[0:1]
 
+    def sums(owner, part, total):
+        base = owner * fine_dev + part * half
+        start = (first_tile[0, owner], other_first[0, 0, owner])
+        total[...] = jnp.zeros_like(total)
+        hits[...] = jnp.zeros_like(hits)
+
+        def rows_of(side, tile):
+            return (emb, other_emb)[side][start[side] + tile]
+
+        def ids_of(side, tile):
+            return (ids, other_ids)[side][start[side] + tile] - base
+
+        add_tiles(total, rows_of, ids_of, tiles // DEPTH, DEPTH)
+        return hit_row()
+
     sends = []
     for slot, (qx, qy, part) in enumerate(FIRST):
         counts[pl.ds(slot, 1), :] = sums(along[qx, qy], part, acc.at[0])
         if slot == 5:
             count_copies = []
-            for place, (cx, cy) in enumerate(((1, 0), (0, 1), (1, 1))):
+            for place, quad in enumerate(AWAY):
                 copy = remote(
                     counts,
                     landed_counts.at[place],
                     count_send.at[place],
                     count_recv.at[place],
-                    along[cx, cy],
+                    along[quad],
                 )
                 copy.start()
                 count_copies.append(copy)
@@ -151,59 +198,179 @@
         own_counts[pl.ds(part, 1), :] = sums(me, part, acc.at[part])
     for copy in count_copies:
         copy.wait_recv()
+
+    def column(row):
+        return jnp.broadcast_to(row, (LANES, row.shape[1])).T
+
+    fine_swaps = []
     for part in range(2):
         seen = own_counts[pl.ds(part, 1), :]
-        for place, quad in enumerate(((1, 0), (0, 1), (1, 1))):
+        for place, quad in enumerate(AWAY):
             row = FIRST.index(quad + (part,))
             seen = seen + landed_counts[place, pl.ds(row, 1), :]
-        divisor = jnp.broadcast_to(seen + 1.0, (LANES, half)).T
-        divisor = jnp.concatenate([divisor] * (old.shape[1] // LANES), axis=1)
+        divisor = jnp.concatenate([column(seen + 1.0)] * (width // LANES), axis=1)
         near, far = (2, 5) if part == 0 else (3, 4)
         sends[near].wait_recv()
         sends[far].wait_recv()
-        span = pl.ds(part * half, half)
         total = acc[part] + landed[near].astype(jnp.float32) + landed[far].astype(jnp.float32)
-        out[span, :] = ((total + old[span, :].astype(jnp.float32)) / divisor).astype(jnp.bfloat16)
-    for copy in swaps + sends + count_copies:
+        total = total + old[pl.ds(part * half, half), :].astype(jnp.float32)
+        span = pl.ds(part * (fine_tiles // 2), fine_tiles // 2)
+        out[span] = (total / divisor).astype(jnp.bfloat16).reshape(-1, LANES, width)
+        copy = remote(
+            out.at[span], other_fine.at[span], fine_send.at[part], fine_recv.at[part], partner
+        )
+        copy.start()
+        fine_swaps.append(copy)
+
+    quads = AWAY + ((0, 0),)
+    acc[0] = jnp.zeros_like(acc[0])
+    hits[...] = jnp.zeros_like(hits)
+    for copy in fine_swaps:
+        copy.wait_recv()
+
+    def place_of(coarse):
+        owner = coarse // coarse_dev
+        row = jnp.full_like(coarse, -1)
+        for order, quad in enumerate(quads):
+            inside = coarse - along[quad] * coarse_dev
+            row = jnp.where(owner == along[quad], inside + order * coarse_dev, row)
+        return row
+
+    def fine_rows(side, tile):
+        return (out, other_fine)[side][tile]
+
+    def coarse_places(side, tile):
+        return place_of((ids, other_ids)[side][label_rows + META + tile])
+
+    add_tiles(acc.at[0], fine_rows, coarse_places, fine_tiles // DEPTH, DEPTH)
+    coarse_counts[pl.ds(0, 1), :] = hit_row()
+    coarse_copies = []
+    for order, quad in enumerate(AWAY):
+        coarse_away[order] = acc[0, pl.ds(order * coarse_dev, coarse_dev), :].astype(jnp.bfloat16)
+        for copy in (
+            remote(
+                coarse_counts,
+                coarse_counts_landed.at[order],
+                coarse_count_send.at[order],
+                coarse_count_recv.at[order],
+                along[quad],
+            ),
+            remote(
+                coarse_away.at[order],
+                coarse_landed.at[order],
+                coarse_send.at[order],
+                coarse_recv.at[order],
+                along[quad],
+            ),
+        ):
+            copy.start()
+            coarse_copies.append(copy)
+    total = acc[0, pl.ds(3 * coarse_dev, coarse_dev), :] + old_coarse[...].astype(jnp.float32)
+    seen = coarse_counts[pl.ds(0, 1), pl.ds(3 * coarse_dev, coarse_dev)]
+    for copy in coarse_copies:
+        copy.wait_recv()
+    for order in range(3):
+        total = total + coarse_landed[order].astype(jnp.float32)
+        seen = seen + coarse_counts_landed[order, pl.ds(0, 1), pl.ds(order * coarse_dev, coarse_dev)]
+    mean = total / jnp.concatenate([column(seen + 1.0)] * (width // LANES), axis=1)
+    means[slab] = mean.astype(jnp.bfloat16)
+    square = jnp.sum(mean * mean, axis=1, keepdims=True)
+    squares[slab] = jnp.broadcast_to(square, (coarse_dev, LANES)).T[0:8]
+    mean_copies = []
+    for order, other in enumerate(others):
+        for copy in (
+            remote(
+                squares.at[slab],
+                squares.at[slab],
+                squares_send.at[order],
+                squares_recv.at[order],
+                other,
+                "grp",
+            ),
+            remote(
+                means.at[slab],
+                means.at[slab],
+                means_send.at[order],
+                means_recv.at[order],
+                other,
+                "grp",
+            ),
+        ):
+            copy.start()
+            mean_copies.append(copy)
+    for copy in mean_copies:
+        copy.wait_recv()
+    square = squares[0, 0:1]
+    for at in range(1, slabs):
+        square = square + squares[at, 0:1]
+    scale = column(lax.rsqrt(square / (width * slabs) + 1e-06))
+    scale = jnp.concatenate([scale] * (width // LANES), axis=1)
+    for at in range(slabs):
+        dirs[:, at * width : (at + 1) * width] = (means[at].astype(jnp.float32) * scale).astype(
+            jnp.bfloat16
+        )
+    for copy in swaps + sends + count_copies + fine_swaps + coarse_copies + mean_copies:
         copy.wait_send()
 
 
-def fine_level(embeddings, fine_local, send_counts, old_fine):
+DEPTH = 2
+
+
+def tree_levels(embeddings, fine_local, send_counts, old_fine, coarse_ids, old_coarse):
     peers = lax.axis_size("rows")
+    slabs = lax.axis_size("grp")
     per_dev, width = embeddings.shape
     fine_dev = old_fine.shape[0]
+    coarse_dev = old_coarse.shape[0]
     half = fine_dev // 2
     capacity = 2 * per_dev // peers
-    tiles = capacity // LANES + 1
+    tiles = -(-(capacity // LANES + 1) // DEPTH) * DEPTH
     position = jnp.arange(per_dev, dtype=jnp.int32)
     before = jnp.arange(peers)[None, :] < jnp.arange(peers)[:, None]
     starts = jnp.sum(jnp.where(before, send_counts, 0), axis=1)
     ends = starts + send_counts[0]
     owner = jnp.sum((ends[:, None] <= position[None, :]).astype(jnp.int32), axis=0)
     label_rows = per_dev // LANES
+    fine_tiles = fine_dev // LANES
     first_tile = jnp.minimum(starts // LANES, label_rows - tiles)[None, :]
-    gid = (owner * fine_dev + fine_local).reshape(label_rows, LANES)
-    gid = jnp.concatenate([gid, jnp.pad(first_tile, ((0, 7), (0, LANES - peers)))], axis=0)
-    gid = gid[:, None, :]
+    ids = jnp.concatenate(
+        [
+            (owner * fine_dev + fine_local).reshape(label_rows, LANES),
+            jnp.pad(first_tile, ((0, META - 1), (0, LANES - peers))),
+            coarse_ids.reshape(fine_tiles, LANES),
+        ],
+        axis=0,
+    )[:, None, :]
     tiled = embeddings.reshape(label_rows, LANES, width)
     vmem = pl.BlockSpec(memory_space=pltpu.VMEM)
     dma = pltpu.SemaphoreType.DMA
-    return pl.pallas_call(
-        functools.partial(fine_kernel, tiles),
-        out_shape=jax.ShapeDtypeStruct(old_fine.shape, jnp.bfloat16),
-        in_specs=[vmem, vmem, pl.BlockSpec(memory_space=pltpu.SMEM), vmem],
-        out_specs=vmem,
+    f32, bf16 = jnp.float32, jnp.bfloat16
+    new_fine, dirs = pl.pallas_call(
+        functools.partial(levels_kernel, tiles),
+        out_shape=[
+            jax.ShapeDtypeStruct((fine_tiles, LANES, width), bf16),
+            jax.ShapeDtypeStruct((coarse_dev, slabs * width), bf16),
+        ],
+        in_specs=[vmem, vmem, pl.BlockSpec(memory_space=pltpu.SMEM), vmem, vmem],
+        out_specs=[vmem, vmem],
         scratch_shapes=[
-            pltpu.VMEM(tiled.shape, jnp.bfloat16),
-            pltpu.VMEM(gid.shape, jnp.int32),
-            pltpu.SMEM((8, 1, LANES), jnp.int32),
-            pltpu.VMEM((2, half, width), jnp.float32),
-            pltpu.VMEM((half, LANES), jnp.bfloat16),
-            pltpu.VMEM((6, half, width), jnp.bfloat16),
-            pltpu.VMEM((6, half, width), jnp.bfloat16),
-            pltpu.VMEM((8, half), jnp.float32),
-            pltpu.VMEM((8, half), jnp.float32),
-            pltpu.VMEM((3, 8, half), jnp.float32),
+            pltpu.VMEM(tiled.shape, bf16),
+            pltpu.VMEM(ids.shape, jnp.int32),
+            pltpu.SMEM((META, 1, LANES), jnp.int32),
+            pltpu.VMEM((2, half, width), f32),
+            pltpu.VMEM((half, LANES), bf16),
+            pltpu.VMEM((6, half, width), bf16),
+            pltpu.VMEM((6, half, width), bf16),
+            pltpu.VMEM((8, half), f32),
+            pltpu.VMEM((8, half), f32),
+            pltpu.VMEM((3, 8, half), f32),
+            pltpu.VMEM((fine_tiles, LANES, width), bf16),
+            pltpu.VMEM((3, coarse_dev, width), bf16),
+            pltpu.VMEM((3, coarse_dev, width), bf16),
+            pltpu.VMEM((8, half), f32),
+            pltpu.VMEM((3, 8, half), f32),
+            pltpu.VMEM((slabs, coarse_dev, width), bf16),
+            pltpu.VMEM((slabs, 8, coarse_dev), f32),
             dma((2,)),
             dma((2,)),
             dma,
@@ -211,11 +378,22 @@
             dma((6,)),
             dma((3,)),
             dma((3,)),
+            dma((2,)),
+            dma((2,)),
+            dma((3,)),
+            dma((3,)),
+            dma((3,)),
+            dma((3,)),
+            dma((slabs - 1,)),
+            dma((slabs - 1,)),
+            dma((slabs - 1,)),
+            dma((slabs - 1,)),
         ],
         compiler_params=pltpu.CompilerParams(
             collective_id=0, has_side_effects=True, vmem_limit_bytes=48 * 1024 * 1024
         ),
-    )(tiled, gid, first_tile, old_fine)
+    )(tiled, ids, first_tile, old_fine, old_coarse)
+    return new_fine.reshape(old_fine.shape), dirs
 
 
 def onehot_sums(arrived, arrived_labels, fine_dev):
@@ -288,9 +466,10 @@
     quarter = embeddings.shape[1]
     fine_dev = old_fine.shape[0]
     coarse_dev = old_coarse.shape[0]
-    tree = peer_count == 8 and 2 * embeddings.shape[0] // peer_count >= fine_dev
-    level = fine_level if tree else exchanged_rows
-    new_fine = level(embeddings, fine_local, send_counts, old_fine)
+    dense = 2 * embeddings.shape[0] // peer_count >= fine_dev
+    if peer_count == 8 and dense and 8 * coarse_dev == fine_dev:
+        return tree_levels(embeddings, fine_local, send_counts, old_fine, coarse_ids, old_coarse)
+    new_fine = exchanged_rows(embeddings, fine_local, send_counts, old_fine)
     owners = coarse_ids // coarse_dev
     local_id = coarse_ids - owners * coarse_dev
     capacity_two = 2 * fine_dev // peer_count

time: 159 us -> 98.3 us (0.62)
  blocking collectives: 28 us -> 0 us
  waiting for transfers between devices: 25.4 us -> 0 us
  Pallas kernels: 71.3 us -> 90.3 us
  matrix products: 15.6 us -> 0 us
  starting transfers between devices: 8.91 us -> 0 us
  other arithmetic: 6.03 us -> 3.07 us
    all_to_all x2 -> x0, waiting for transfers between devices: 25.4 us -> none  [the longest x1 25.4 us: on_device(): lax.all_to_all(outgoing_two.reshape(peer_count, capacity_two, quarter), '...]
    pallas_call x1, Pallas kernels: 71.3 us -> 90.3 us  [tree_levels(): pl.pallas_call(functools.partial(levels_kernel, tiles), out_shape=[jax.Sh...]
    all_gather x1 -> x0, blocking collectives: 15.9 us -> none  [on_device(): coarse_dirs = lax.all_gather(unit_part, 'grp', axis=1, tiled=True)]
    dot_general x3 -> x0, matrix products: 15.6 us -> none  [the longest x1 7.47 us: on_device(): jnp.dot(placement, new_fine, preferred_element_type=jnp.float32)]
    psum x1 -> x0, blocking collectives: 12.1 us -> none  [on_device(): squares = lax.psum(jnp.sum(coarse_means * coarse_means, axis=1), 'grp')]
    all_to_all x2 -> x0, starting transfers between devices: 8.91 us -> none  [the longest x1 5.17 us: on_device(): lax.all_to_all(labels_two.reshape(peer_count, capacity_two), 'rows', spli...]
    another operation x2 -> x0, other arithmetic: 2.45 us -> none
    unnamed x11 -> x6, local copies, waits for them, and re-layouts: 2.09 us -> 3.89 us
  transfers between devices with their start and end apart: 2 -> 0, of which waited for: 1 -> 0; matrix products, arithmetic and copies ran while one was open for 6% -> 0% of each run, Pallas kernels for 45% -> 0%
where the time goes in v2:
time: 98.3 us; the launch traced here: 98 us
  Pallas kernels  90.3 us (92%)
  local copies, waits for them, and re-layouts  3.89 us (4%)
  other arithmetic  3.07 us (3%)
    pallas_call x1, Pallas kernels, tree_levels(): pl.pallas_call(functools.partial(levels_kernel, tiles), out_shape=[jax.Sh...  90.3 us
    unnamed x6, local copies, waits for them, and re-layouts  3.89 us

profile of v2, /device:TPU:0, one launch (start us, length us, event | category | flops | bytes accessed | tf_op | source)
XLA Modules:
  0.0 98.0 jit_solution(1613515722112309090)
XLA Ops:
  0.6 0.8 select_reduce_fusion
  1.4 0.7 bitcast_add_fusion
  2.1 0.2 convert_reduce_fusion
  2.2 0.8 add_bitcast_fusion
  3.0 0.7 fusion
  3.7 0.0 copy-start
  3.7 1.2 %copy-done = bf16[2048,256]{1,0:T(8,128)(2,1)S(1)} copy-done((bf16[2048,256]{1,0:T(8,128)(2,1)S(1)}, bf16[2048,256]{1,0:T(8,128)(2,1)}, u32[]{:S(2)}) %copy-start) | copy-done | bytes 1048600
  4.9 0.0 copy-start.1
  4.9 0.9 copy-done.1
  5.8 90.3 %shard_map.77 = (bf16[16,128,256]{2,1,0:T(8,128)(2,1)S(1)}, bf16[256,1024]{1,0:T(8,128)(2,1)S(1)}) custom-call(bf16[64,128,256]{2,1,0:T(8,128)(2,1)} %bitcast.20, s32[88,1,128]{2,1,0:T(1,128)S(1)} %bitcast.19, s32[1,8]{1,0:T(1,128)S(1)} %fusion.1.first_tile, bf16[2048,256]{1,0:T(8,128)(2,1)S(1)} %copy-done, bf16[256,256]{1,0:T(8,128)(2,1)S(1)} %copy-done.1), custom_call_target="tpu_custom_call" | custom-call | tf_op jit(solution)/shard_map/pallas_call | solution.py:348
  96.2 1.0 copy.10
  97.2 0.8 copy.11
  (1 shorter events, 0.0 us)
Async XLA Ops:
  3.7 1.2 %copy-start = (bf16[2048,256]{1,0:T(8,128)(2,1)S(1)}, bf16[2048,256]{1,0:T(8,128)(2,1)}, u32[]{:S(2)}) copy-start(bf16[2048,256]{1,0:T(8,128)(2,1)} %old.1) | copy-start | bytes 3145732
  4.9 0.9 copy-start.1

commit v3 on v2

--- a/solution.py
+++ b/solution.py
@@ -28,6 +28,8 @@
 FIRST = ((1, 1, 0), (1, 1, 1), (1, 0, 0), (0, 1, 1), (1, 0, 1), (0, 1, 0))
 AWAY = ((1, 1), (1, 0), (0, 1))
 META = 8
+FINE_DEPTH = 9
+COARSE_DEPTH = 8
 
 
 def one_hot(index, ids):
@@ -39,14 +41,17 @@
 def levels_kernel(
     tiles,
     emb,
-    ids,
-    first_tile,
+    fine_local,
+    sent,
+    coarse_ids,
     old,
     old_coarse,
     out,
     dirs,
     other_emb,
+    ids,
     other_ids,
+    first_tile,
     other_first,
     acc,
     hits,
@@ -113,66 +118,84 @@
         remote(ids, other_ids, swap_send.at[0], swap_recv.at[0], partner),
         remote(emb, other_emb, swap_send.at[1], swap_recv.at[1], partner),
     ]
-    for copy in swaps:
-        copy.start()
+    swaps[1].start()
+    place = lax.broadcasted_iota(jnp.int32, fine_local.shape, 0) * LANES
+    place = place + lax.broadcasted_iota(jnp.int32, fine_local.shape, 2)
+    lane = lax.broadcasted_iota(jnp.int32, (1, LANES), 1)
+    owner = jnp.zeros_like(place)
+    first = jnp.zeros_like(lane)
+    end = 0
+    for peer in range(sent.shape[1]):
+        tile = jnp.minimum(end // LANES, label_rows - tiles)
+        first_tile[peer] = tile
+        first = jnp.where(lane == peer, tile, first)
+        end = end + sent[0, peer]
+        owner = owner + jnp.where(end <= place, 1, 0)
+    ids[pl.ds(0, label_rows)] = owner * fine_dev + fine_local[...]
+    ids[pl.ds(label_rows, META)] = jnp.zeros((META, 1, LANES), jnp.int32)
+    ids[label_rows] = first
+    ids[pl.ds(label_rows + META, fine_tiles)] = coarse_ids[...]
+    swaps[0].start()
     counts[...] = jnp.zeros_like(counts)
     coarse_counts[...] = jnp.zeros_like(coarse_counts)
+    index = lax.broadcasted_iota(jnp.int32, (half, LANES), 0).astype(jnp.int16)
+
+    def add_tiles(total, hit, rows_of, ids_of, steps, depth, sides):
+        @pl.loop(0, steps)
+        def _(step):
+            hots, rows = [], []
+            for part in range(depth):
+                for side in sides:
+                    hots.append(one_hot(index, ids_of(side, step * depth + part)))
+                    rows.append(rows_of(side, step * depth + part))
+            hit[...] += functools.reduce(jnp.add, hots)
+            total[...] += jnp.dot(
+                jnp.concatenate(hots, axis=1),
+                jnp.concatenate(rows, axis=0),
+                preferred_element_type=jnp.float32,
+            )
+
+    def hit_row(hit):
+        return lax.dot_general(
+            jnp.ones((8, LANES), jnp.bfloat16),
+            hit[...],
+            (((1,), (1,)), ((), ())),
+            preferred_element_type=jnp.float32,
+        )[0:1]
+
+    def add_rows(owner, part, total, hit, sides):
+        base = owner * fine_dev + part * half
+
+        def start_of(side):
+            return first_tile[owner] if side == 0 else other_first[0, 0, owner]
+
+        start = {side: start_of(side) for side in sides}
+
+        def rows_of(side, tile):
+            return (emb, other_emb)[side][start[side] + tile]
+
+        def ids_of(side, tile):
+            return (ids, other_ids)[side][start[side] + tile] - base
+
+        if 0 in sides:
+            total[...] = jnp.zeros_like(total)
+            hit[...] = jnp.zeros_like(hit)
+        add_tiles(total, hit, rows_of, ids_of, tiles // FINE_DEPTH, FINE_DEPTH, sides)
+
+    for slot, (qx, qy, part) in enumerate(FIRST[:2]):
+        add_rows(along[qx, qy], part, acc.at[slot], hits.at[slot], (0,))
     swaps[0].wait_recv()
     meta = pltpu.make_async_copy(other_ids.at[pl.ds(label_rows, META)], other_first, meta_sem)
     meta.start()
     meta.wait()
     swaps[1].wait_recv()
 
-    index = lax.broadcasted_iota(jnp.int32, (half, LANES), 0).astype(jnp.int16)
-
-    def add_tiles(total, rows_of, ids_of, steps, depth):
-        def piece(tile):
-            hots, rows = [], []
-            for side in range(2):
-                hots.append(one_hot(index, ids_of(side, tile)))
-                rows.append(rows_of(side, tile))
-            hits[...] += hots[0] + hots[1]
-            return hots, rows
-
-        @pl.loop(0, steps)
-        def _(step):
-            hots, rows = [], []
-            for part in range(depth):
-                more_hots, more_rows = piece(step * depth + part)
-                hots += more_hots
-                rows += more_rows
-            total[...] += jnp.dot(
-                jnp.concatenate(hots, axis=1),
-                jnp.concatenate(rows, axis=0),
-                preferred_element_type=jnp.float32,
-            )
-
-    def hit_row():
-        return lax.dot_general(
-            jnp.ones((8, LANES), jnp.bfloat16),
-            hits[...],
-            (((1,), (1,)), ((), ())),
-            preferred_element_type=jnp.float32,
-        )[0:1]
-
-    def sums(owner, part, total):
-        base = owner * fine_dev + part * half
-        start = (first_tile[0, owner], other_first[0, 0, owner])
-        total[...] = jnp.zeros_like(total)
-        hits[...] = jnp.zeros_like(hits)
-
-        def rows_of(side, tile):
-            return (emb, other_emb)[side][start[side] + tile]
-
-        def ids_of(side, tile):
-            return (ids, other_ids)[side][start[side] + tile] - base
-
-        add_tiles(total, rows_of, ids_of, tiles // DEPTH, DEPTH)
-        return hit_row()
-
     sends = []
     for slot, (qx, qy, part) in enumerate(FIRST):
-        counts[pl.ds(slot, 1), :] = sums(along[qx, qy], part, acc.at[0])
+        at = slot if slot < 2 else 0
+        sides = (1,) if slot < 2 else (0, 1)
+        add_rows(along[qx, qy], part, acc.at[at], hits.at[at], sides)
+        counts[pl.ds(slot, 1), :] = hit_row(hits.at[at])
         if slot == 5:
             count_copies = []
             for place, quad in enumerate(AWAY):
@@ -189,13 +212,14 @@
             sends[5 - slot].wait_recv()
             away[slot] = (acc[0] + landed[5 - slot].astype(jnp.float32)).astype(jnp.bfloat16)
         else:
-            away[slot] = acc[0].astype(jnp.bfloat16)
+            away[slot] = acc[at].astype(jnp.bfloat16)
         target = along[1, 0] if slot % 2 == 0 else along[0, 1]
         copy = remote(away.at[slot], landed.at[slot], send_sem.at[slot], recv_sem.at[slot], target)
         copy.start()
         sends.append(copy)
     for part in range(2):
-        own_counts[pl.ds(part, 1), :] = sums(me, part, acc.at[part])
+        add_rows(me, part, acc.at[part], hits.at[0], (0, 1))
+        own_counts[pl.ds(part, 1), :] = hit_row(hits.at[0])
     for copy in count_copies:
         copy.wait_recv()
 
@@ -224,7 +248,7 @@
 
     quads = AWAY + ((0, 0),)
     acc[0] = jnp.zeros_like(acc[0])
-    hits[...] = jnp.zeros_like(hits)
+    hits[0] = jnp.zeros_like(hits[0])
     for copy in fine_swaps:
         copy.wait_recv()
 
@@ -242,8 +266,9 @@
     def coarse_places(side, tile):
         return place_of((ids, other_ids)[side][label_rows + META + tile])
 
-    add_tiles(acc.at[0], fine_rows, coarse_places, fine_tiles // DEPTH, DEPTH)
-    coarse_counts[pl.ds(0, 1), :] = hit_row()
+    steps = fine_tiles // COARSE_DEPTH
+    add_tiles(acc.at[0], hits.at[0], fine_rows, coarse_places, steps, COARSE_DEPTH, (0, 1))
+    coarse_counts[pl.ds(0, 1), :] = hit_row(hits.at[0])
     coarse_copies = []
     for order, quad in enumerate(AWAY):
         coarse_away[order] = acc[0, pl.ds(order * coarse_dev, coarse_dev), :].astype(jnp.bfloat16)
@@ -313,9 +338,6 @@
         copy.wait_send()
 
 
-DEPTH = 2
-
-
 def tree_levels(embeddings, fine_local, send_counts, old_fine, coarse_ids, old_coarse):
     peers = lax.axis_size("rows")
     slabs = lax.axis_size("grp")
@@ -324,23 +346,10 @@
     coarse_dev = old_coarse.shape[0]
     half = fine_dev // 2
     capacity = 2 * per_dev // peers
-    tiles = -(-(capacity // LANES + 1) // DEPTH) * DEPTH
-    position = jnp.arange(per_dev, dtype=jnp.int32)
-    before = jnp.arange(peers)[None, :] < jnp.arange(peers)[:, None]
-    starts = jnp.sum(jnp.where(before, send_counts, 0), axis=1)
-    ends = starts + send_counts[0]
-    owner = jnp.sum((ends[:, None] <= position[None, :]).astype(jnp.int32), axis=0)
+    tiles = -(-(capacity // LANES + 1) // FINE_DEPTH) * FINE_DEPTH
     label_rows = per_dev // LANES
     fine_tiles = fine_dev // LANES
-    first_tile = jnp.minimum(starts // LANES, label_rows - tiles)[None, :]
-    ids = jnp.concatenate(
-        [
-            (owner * fine_dev + fine_local).reshape(label_rows, LANES),
-            jnp.pad(first_tile, ((0, META - 1), (0, LANES - peers))),
-            coarse_ids.reshape(fine_tiles, LANES),
-        ],
-        axis=0,
-    )[:, None, :]
+    id_shape = (label_rows + META + fine_tiles, 1, LANES)
     tiled = embeddings.reshape(label_rows, LANES, width)
     vmem = pl.BlockSpec(memory_space=pltpu.VMEM)
     dma = pltpu.SemaphoreType.DMA
@@ -351,14 +360,16 @@
             jax.ShapeDtypeStruct((fine_tiles, LANES, width), bf16),
             jax.ShapeDtypeStruct((coarse_dev, slabs * width), bf16),
         ],
-        in_specs=[vmem, vmem, pl.BlockSpec(memory_space=pltpu.SMEM), vmem, vmem],
+        in_specs=[vmem, vmem, pl.BlockSpec(memory_space=pltpu.SMEM), vmem, vmem, vmem],
         out_specs=[vmem, vmem],
         scratch_shapes=[
             pltpu.VMEM(tiled.shape, bf16),
-            pltpu.VMEM(ids.shape, jnp.int32),
+            pltpu.VMEM(id_shape, jnp.int32),
+            pltpu.VMEM(id_shape, jnp.int32),
+            pltpu.SMEM((peers,), jnp.int32),
             pltpu.SMEM((META, 1, LANES), jnp.int32),
             pltpu.VMEM((2, half, width), f32),
-            pltpu.VMEM((half, LANES), bf16),
+            pltpu.VMEM((2, half, LANES), bf16),
             pltpu.VMEM((6, half, width), bf16),
             pltpu.VMEM((6, half, width), bf16),
             pltpu.VMEM((8, half), f32),
@@ -392,7 +403,14 @@
         compiler_params=pltpu.CompilerParams(
             collective_id=0, has_side_effects=True, vmem_limit_bytes=48 * 1024 * 1024
         ),
-    )(tiled, ids, first_tile, old_fine, old_coarse)
+    )(
+        tiled,
+        fine_local.reshape(label_rows, 1, LANES),
+        send_counts,
+        coarse_ids.reshape(fine_tiles, 1, LANES),
+        old_fine,
+        old_coarse,
+    )
     return new_fine.reshape(old_fine.shape), dirs
 
 

time: 98.3 us -> 90.5 us (0.921)
  Pallas kernels: 90.3 us -> 83.6 us
  other arithmetic: 3.07 us -> 0 us
  local copies, waits for them, and re-layouts: 3.89 us -> 6 us
    pallas_call x1, Pallas kernels: 90.3 us -> 83.6 us  [tree_levels(): pl.pallas_call(functools.partial(levels_kernel, tiles), out_shape=[jax.Sh...]
    unnamed x6 -> x12, local copies, waits for them, and re-layouts: 3.89 us -> 6 us
where the time goes in v3:
time: 90.5 us; the launch traced here: 90.2 us
  Pallas kernels  83.6 us (92%)
  local copies, waits for them, and re-layouts  6 us (7%)
    pallas_call x1, Pallas kernels, tree_levels(): pl.pallas_call(functools.partial(levels_kernel, tiles), out_shape=[jax.Sh...  83.6 us
    unnamed x12, local copies, waits for them, and re-layouts  6 us

profile of v3, /device:TPU:0, one launch (start us, length us, event | category | flops | bytes accessed | tf_op | source)
XLA Modules:
  0.0 90.2 jit_solution(12391057065778087957)
XLA Ops:
  0.6 0.0 copy-start
  0.6 1.2 %copy-done = bf16[2048,256]{1,0:T(8,128)(2,1)S(1)} copy-done((bf16[2048,256]{1,0:T(8,128)(2,1)S(1)}, bf16[2048,256]{1,0:T(8,128)(2,1)}, u32[]{:S(2)}) %copy-start) | copy-done | bytes 1048600
  1.9 0.0 copy-start.1
  1.9 0.9 copy-done.1
  2.8 0.0 copy-start.2
  2.8 0.8 copy-done.2
  3.5 0.0 copy-start.3
  3.5 0.7 copy-done.3
  4.2 0.0 copy-start.4
  4.2 0.7 copy-done.4
  4.9 83.6 %shard_map.77 = (bf16[16,128,256]{2,1,0:T(8,128)(2,1)S(1)}, bf16[256,1024]{1,0:T(8,128)(2,1)S(1)}) custom-call(bf16[64,128,256]{2,1,0:T(8,128)(2,1)} %bitcast.7, s32[64,1,128]{2,1,0:T(1,128)S(1)} %bitcast.5, s32[1,8]{1,0:T(1,128)S(1)} %copy-done.4, s32[16,1,128]{2,1,0:T(1,128)S(1)} %bitcast.6, bf16[2048,256]{1,0:T(8,128)(2,1)S(1)} %copy-done, ...), custom_call_target="tpu_custom_call" | custom-call | tf_op jit(solution)/shard_map/pallas_call | solution.py:357
  88.4 1.0 %copy.10 = bf16[2048,256]{1,0:T(8,128)(2,1)} copy(bf16[2048,256]{1,0:T(8,128)(2,1)S(1)} %bitcast.4) | data formatting | bytes 2097152
  89.4 0.8 copy.11
Async XLA Ops:
  0.6 1.2 %copy-start = (bf16[2048,256]{1,0:T(8,128)(2,1)S(1)}, bf16[2048,256]{1,0:T(8,128)(2,1)}, u32[]{:S(2)}) copy-start(bf16[2048,256]{1,0:T(8,128)(2,1)} %old.1) | copy-start | bytes 3145732
  1.9 0.9 %copy-start.1 = (bf16[256,256]{1,0:T(8,128)(2,1)S(1)}, bf16[256,256]{1,0:T(8,128)(2,1)}, u32[]{:S(2)}) copy-start(bf16[256,256]{1,0:T(8,128)(2,1)} %old_coarse.1) | copy-start | bytes 393220
  2.8 0.8 copy-start.2
  3.5 0.7 copy-start.3
  4.2 0.7 copy-start.4
